TPU v7x, 128 devices: a whole 4x4x4 slice. The times are simulated.
128 devices in a mesh: doc: 4 (over y), resp: 8 (over z, x_hi), prob: 4 (over x_lo, core).
Axes of the slice: x: 4 (x_hi: 2, x_lo: 2; x = x_hi * 2 + x_lo), y: 4, z: 4, core: 2. Of those that a mesh axis runs over, the one named last changes fastest.
Arguments:
- x_doc: bfloat16 [512, 5120], P('doc'), may hold values from -6 to 6
- x_prompt: bfloat16 [4, 1024, 5120], P('prob', 'resp'), may hold values from -6 to 6
- w_key: bfloat16 [5120, 512], replicated, may hold values from -0.078125 to 0.078125
- w_value: bfloat16 [5120, 512], replicated, may hold values from -0.078125 to 0.078125
- queries: bfloat16 [128, 128, 4096], P(('doc', 'resp', 'prob')), may hold values from -240 to 240
- resp_keys: bfloat16 [128, 128, 512], P(('doc', 'resp', 'prob')), may hold values from -6 to 6
- resp_values: bfloat16 [128, 128, 512], P(('doc', 'resp', 'prob')), may hold values from -6 to 6
- out_grad: bfloat16 [128, 128, 4096], P(('doc', 'resp', 'prob')), may hold values from -6 to 6
- lengths: int32 [128], P(('doc', 'resp', 'prob')), may hold values from 64 to 128, as said below
Outputs:
- grad_queries: bfloat16 [128, 128, 4096], P(('doc', 'resp', 'prob'))
- grad_keys: bfloat16 [128, 128, 512], P(('doc', 'resp', 'prob'))
- grad_values: bfloat16 [128, 128, 512], P(('doc', 'resp', 'prob'))
- grad_doc: bfloat16 [512, 5120], P('doc')
- grad_prompt: bfloat16 [4, 1024, 5120], P('prob', 'resp')
Inputs may be any that keep to these rules, and one draw needn't show every extreme that they name: `lengths`: token slots at or beyond a response's length are padding.
All inputs are finite; a program needn't handle non-finite values.
Results may differ from a plain program's by a relative error of at most 0.0085.
Values may be sent and summed in bfloat16 or wider, within the bound.
No kernel may reach another device: no remote copies, remote signals or barrier semaphores. Data moves between devices by JAX's collectives and lax.ppermute only.
A program may use at most 128 MiB of HBM per device.

v0:
```python
import jax
import jax.numpy as jnp
from jax import lax
from jax.sharding import PartitionSpec as P

QH = 32
KVH = 4
HD = 128
R = 128


def back_project(pair, w_key, w_value):
    first = lax.dot_general(
        pair[0], w_key, (((1,), (1,)), ((), ())), preferred_element_type=jnp.float32
    )
    second = lax.dot_general(
        pair[1], w_value, (((1,), (1,)), ((), ())), preferred_element_type=jnp.float32
    )
    return (first + second).astype(jnp.bfloat16)


def on_device(x_doc, x_prompt, w_key, w_value, queries, resp_keys, resp_values, out_grad, lengths):
    scale = 1.0 / HD**0.5
    width = KVH * HD
    group = QH // KVH
    doc_pair = jnp.stack(
        [
            jnp.dot(x_doc, w_key, preferred_element_type=jnp.float32).astype(jnp.bfloat16),
            jnp.dot(x_doc, w_value, preferred_element_type=jnp.float32).astype(jnp.bfloat16),
        ]
    )
    doc_full = lax.all_gather(doc_pair, "doc", axis=1, tiled=True)
    prompt_rows = x_prompt[0]
    prompt_pair = jnp.stack(
        [
            jnp.dot(prompt_rows, w_key, preferred_element_type=jnp.float32).astype(jnp.bfloat16),
            jnp.dot(prompt_rows, w_value, preferred_element_type=jnp.float32).astype(jnp.bfloat16),
        ]
    )
    prompt_full = lax.all_gather(prompt_pair, "resp", axis=1, tiled=True)
    doc_len = doc_full.shape[1]
    prompt_len = prompt_full.shape[1]
    pre = doc_len + prompt_len
    keys = jnp.concatenate([doc_full[0], prompt_full[0], resp_keys[0]], axis=0)
    values = jnp.concatenate([doc_full[1], prompt_full[1], resp_values[0]], axis=0)
    total_keys = keys.shape[0]
    length = lengths[0]
    rows = jnp.arange(R, dtype=jnp.int32)
    cols = jnp.arange(total_keys, dtype=jnp.int32)
    later = cols - pre
    allowed = (cols[None, :] < pre) | (later[None, :] <= rows[:, None]) & (later[None, :] < length)
    cot = jnp.where((rows < length)[:, None], out_grad[0], jnp.zeros_like(out_grad[0]))
    q_heads = queries[0].reshape(R, KVH, group, HD).transpose(1, 0, 2, 3)
    cot_heads = cot.reshape(R, KVH, group, HD).transpose(1, 0, 2, 3)
    key_heads = keys.reshape(total_keys, KVH, HD).transpose(1, 0, 2)
    value_heads = values.reshape(total_keys, KVH, HD).transpose(1, 0, 2)

    def per_head(operands):
        qg, gg, kg, vg = operands
        scores = jnp.einsum("tgd,kd->gtk", qg, kg, preferred_element_type=jnp.float32) * scale
        scores = jnp.where(allowed[None], scores, -1e30)
        peak = jnp.max(scores, axis=-1, keepdims=True)
        expo = jnp.exp(scores - peak)
        probs = expo / jnp.sum(expo, axis=-1, keepdims=True)
        probs_b = probs.astype(jnp.bfloat16)
        dprob = jnp.einsum("tgd,kd->gtk", gg, vg, preferred_element_type=jnp.float32)
        delta = jnp.sum(probs * dprob, axis=-1, keepdims=True)
        dscore = (probs * (dprob - delta) * scale).astype(jnp.bfloat16)
        dq = jnp.einsum("gtk,kd->tgd", dscore, kg, preferred_element_type=jnp.float32).astype(
            jnp.bfloat16
        )
        dk = jnp.einsum("gtk,tgd->kd", dscore, qg, preferred_element_type=jnp.float32)
        dv = jnp.einsum("gtk,tgd->kd", probs_b, gg, preferred_element_type=jnp.float32)
        return (dq, dk, dv)

    dq_all, dk_all, dv_all = lax.map(per_head, (q_heads, cot_heads, key_heads, value_heads))
    grad_queries = dq_all.transpose(1, 0, 2, 3).reshape(1, R, QH * HD)
    dk_rows = dk_all.transpose(1, 0, 2).reshape(total_keys, width)
    dv_rows = dv_all.transpose(1, 0, 2).reshape(total_keys, width)
    grad_keys = dk_rows[pre:].astype(jnp.bfloat16)[None]
    grad_values = dv_rows[pre:].astype(jnp.bfloat16)[None]
    doc_terms = jnp.stack([dk_rows[:doc_len], dv_rows[:doc_len]])
    prompt_terms = jnp.stack([dk_rows[doc_len:pre], dv_rows[doc_len:pre]])
    doc_share = lax.psum_scatter(
        doc_terms, ("doc", "resp", "prob"), scatter_dimension=1, tiled=True
    ).astype(jnp.bfloat16)
    doc_sum = lax.all_gather(doc_share, ("resp", "prob"), axis=1, tiled=True)
    n_doc = lax.axis_size("doc")
    n_resp = lax.axis_size("resp")
    ordered = prompt_terms.reshape(2, n_resp, n_doc, prompt_len // (n_resp * n_doc), width)
    ordered = ordered.transpose(0, 2, 1, 3, 4).reshape(2, prompt_len, width)
    prompt_share = lax.psum_scatter(
        ordered, ("doc", "resp"), scatter_dimension=1, tiled=True
    ).astype(jnp.bfloat16)
    prompt_sum = lax.all_gather(prompt_share, "doc", axis=1, tiled=True)
    grad_doc = back_project(doc_sum, w_key, w_value)
    grad_prompt = back_project(prompt_sum, w_key, w_value)[None]
    return (grad_queries, grad_keys, grad_values, grad_doc, grad_prompt)


def solution(mesh):
    placed = (
        P("doc", None),
        P("prob", "resp", None),
        P(),
        P(),
        P(("doc", "resp", "prob"), None, None),
        P(("doc", "resp", "prob"), None, None),
        P(("doc", "resp", "prob"), None, None),
        P(("doc", "resp", "prob"), None, None),
        P(("doc", "resp", "prob")),
    )
    return jax.shard_map(
        on_device,
        mesh=mesh,
        in_specs=placed,
        out_specs=(
            P(("doc", "resp", "prob"), None, None),
            P(("doc", "resp", "prob"), None, None),
            P(("doc", "resp", "prob"), None, None),
            P("doc", None),
            P("prob", "resp", None),
        ),
        check_vma=False,
    )
```

profile of v0, /device:TPU:0, one launch (start us, length us, event | category | flops | bytes accessed | tf_op | source)
XLA Modules:
  0.0 510.8 jit_solution(6242963641408162527)
XLA Ops:
  8.5 3.5 fusion.91
  14.3 3.5 fusion.93
  24.9 15.9 %all-gather.3.cloned.1.call-done = bf16[2,512,512]{2,1,0:T(8,128)(2,1)} async-done(((bf16[2,128,512]{2,1,0:T(8,128)(2,1)}), bf16[2,512,512]{2,1,0:T(8,128)(2,1)}) %all-gather.3.cloned.1.call-update) | async-done | bytes 1048592 | tf_op jit(solution)/shard_map/all_gather | solution.py:32
  44.1 54.1 %all-gather.5.cloned.1.call-done = bf16[2,1024,512]{2,1,0:T(8,128)(2,1)} async-done(((bf16[2,128,512]{2,1,0:T(8,128)(2,1)}), bf16[2,1024,512]{2,1,0:T(8,128)(2,1)}) %all-gather.5.cloned.1.call-update) | async-done | bytes 2097168 | tf_op jit(solution)/shard_map/all_gather | solution.py:40
  106.4 160.1 %while.15 = (s32[]{:T(128)}, bf16[4,128,8,128]{1,3,2,0:T(8,128)(2,1)}, f32[4,1664,128]{1,2,0:T(8,128)}, f32[4,1664,128]{1,2,0:T(8,128)}, bf16[4,1664,128]{2,1,0:...) while((s32[]{:T(128)}, ...), condition=%wide.region_4.5_spmd.clone, body=%wide.region_0.4_spmd.clone.sunk | while | flops 2657216000 | bytes 73817976 | solution.py:76
  107.8 6.2 %fusion.147 = (f32[8,128]{1,0:T(8,128)S(1)}, f32[8,128,1664]{1,2,0:T(8,128)}) fusion(pred[128,1664]{0,1:T(8,128)(4,1)S(1)} %fusion.146, bf16[4,1664,128]{2,1,0:T(8,128)(2,1)} %get-tuple-element.265, s32[]{:T(128)} %get-tuple-element.249, bf16[4,128,8,128]{1,3,2,0:T(8,128)(2,1)} %get-tuple-element.266), kind=kOutput, calls=%fused_computation.100.clone.1 | convolution fusion | flops 443025024 | bytes 7721984 | tf_op jit(solution)/shard_map/while/body/eval_jaxpr/sub | solution.py:63
  114.1 3.9 fusion.145
  117.9 11.7 %fusion.149 = f32[4,1664,128]{1,2,0:T(8,128)} fusion(f32[4,1664,128]{1,2,0:T(8,128)} %get-tuple-element.251, s32[]{:T(128)} %get-tuple-element.249, f32[1664,128,8]{1,0,2:T(8,128)} %fusion.145, bf16[4,128,8,128]{1,3,2,0:T(8,128)(2,1)} %get-tuple-element.266, f32[8,128,1664]{1,2,0:T(8,128)} %get-tuple-element.235, f32[8,128]{1,0:T(8,128)S(1)} %get-tuple-element.236), kind=kOutput, calls=%fused_computation.21.clone.1 | convolution fusion | flops 448137856 | bytes 28386304 | tf_op jit(solution)/shard_map/while/body/eval_jaxpr/gtk,tgd->kd/dot_general | solution.py:72
  129.6 11.7 %fusion.148 = bf16[4,128,8,128]{1,3,2,0:T(8,128)(2,1)} fusion(bf16[4,128,8,128]{1,3,2,0:T(8,128)(2,1)} %get-tuple-element.250, s32[]{:T(128)} %get-tuple-element.249, f32[1664,128,8]{1,0,2:T(8,128)} %fusion.145, bf16[4,1664,128]{2,1,0:T(8,128)(2,1)} %get-tuple-element.265, f32[8,128,1664]{1,2,0:T(8,128)} %get-tuple-element.235, ...), kind=kOutput, calls=%fused_computation.26.clone.1 | convolution fusion | flops 448268928 | bytes 27960320 | tf_op jit(solution)/shard_map/while/body/eval_jaxpr/gtk,kd->tgd/dot_general | solution.py:69
  141.3 5.1 fusion.150
  147.9 6.2 %fusion.147 = (f32[8,128]{1,0:T(8,128)S(1)}, f32[8,128,1664]{1,2,0:T(8,128)}) fusion(pred[128,1664]{0,1:T(8,128)(4,1)S(1)} %fusion.146, bf16[4,1664,128]{2,1,0:T(8,128)(2,1)} %get-tuple-element.265, s32[]{:T(128)} %get-tuple-element.249, bf16[4,128,8,128]{1,3,2,0:T(8,128)(2,1)} %get-tuple-element.266), kind=kOutput, calls=%fused_computation.100.clone.1 | convolution fusion | flops 443025024 | bytes 7721984 | tf_op jit(solution)/shard_map/while/body/eval_jaxpr/sub | solution.py:63
  154.1 3.9 fusion.145
  158.0 11.7 %fusion.149 = f32[4,1664,128]{1,2,0:T(8,128)} fusion(f32[4,1664,128]{1,2,0:T(8,128)} %get-tuple-element.251, s32[]{:T(128)} %get-tuple-element.249, f32[1664,128,8]{1,0,2:T(8,128)} %fusion.145, bf16[4,128,8,128]{1,3,2,0:T(8,128)(2,1)} %get-tuple-element.266, f32[8,128,1664]{1,2,0:T(8,128)} %get-tuple-element.235, f32[8,128]{1,0:T(8,128)S(1)} %get-tuple-element.236), kind=kOutput, calls=%fused_computation.21.clone.1 | convolution fusion | flops 448137856 | bytes 28386304 | tf_op jit(solution)/shard_map/while/body/eval_jaxpr/gtk,tgd->kd/dot_general | solution.py:72
  169.6 11.7 %fusion.148 = bf16[4,128,8,128]{1,3,2,0:T(8,128)(2,1)} fusion(bf16[4,128,8,128]{1,3,2,0:T(8,128)(2,1)} %get-tuple-element.250, s32[]{:T(128)} %get-tuple-element.249, f32[1664,128,8]{1,0,2:T(8,128)} %fusion.145, bf16[4,1664,128]{2,1,0:T(8,128)(2,1)} %get-tuple-element.265, f32[8,128,1664]{1,2,0:T(8,128)} %get-tuple-element.235, ...), kind=kOutput, calls=%fused_computation.26.clone.1 | convolution fusion | flops 448268928 | bytes 27960320 | tf_op jit(solution)/shard_map/while/body/eval_jaxpr/gtk,kd->tgd/dot_general | solution.py:69
  181.3 5.1 %fusion.150 = f32[4,1664,128]{1,2,0:T(8,128)} fusion(f32[4,1664,128]{1,2,0:T(8,128)} %get-tuple-element.252, s32[]{:T(128)} %get-tuple-element.249, bf16[4,128,8,128]{1,3,2,0:T(8,128)(2,1)S(1)} %get-tuple-element.268, f32[8,128]{1,0:T(8,128)S(1)} %get-tuple-element.236, pred[128,1664]{0,1:T(8,128)(4,1)S(1)} %fusion.146, ...), kind=kOutput, calls=%fused_computation.23.clone.1 | convolution fusion | flops 880937600 | bytes 2021376 | tf_op jit(solution)/shard_map/while/body/eval_jaxpr/gtk,tgd->kd/dot_general | solution.py:73
  187.9 6.2 %fusion.147 = (f32[8,128]{1,0:T(8,128)S(1)}, f32[8,128,1664]{1,2,0:T(8,128)}) fusion(pred[128,1664]{0,1:T(8,128)(4,1)S(1)} %fusion.146, bf16[4,1664,128]{2,1,0:T(8,128)(2,1)} %get-tuple-element.265, s32[]{:T(128)} %get-tuple-element.249, bf16[4,128,8,128]{1,3,2,0:T(8,128)(2,1)} %get-tuple-element.266), kind=kOutput, calls=%fused_computation.100.clone.1 | convolution fusion | flops 443025024 | bytes 7721984 | tf_op jit(solution)/shard_map/while/body/eval_jaxpr/sub | solution.py:63
  194.1 3.9 fusion.145
  198.0 11.7 %fusion.149 = f32[4,1664,128]{1,2,0:T(8,128)} fusion(f32[4,1664,128]{1,2,0:T(8,128)} %get-tuple-element.251, s32[]{:T(128)} %get-tuple-element.249, f32[1664,128,8]{1,0,2:T(8,128)} %fusion.145, bf16[4,128,8,128]{1,3,2,0:T(8,128)(2,1)} %get-tuple-element.266, f32[8,128,1664]{1,2,0:T(8,128)} %get-tuple-element.235, f32[8,128]{1,0:T(8,128)S(1)} %get-tuple-element.236), kind=kOutput, calls=%fused_computation.21.clone.1 | convolution fusion | flops 448137856 | bytes 28386304 | tf_op jit(solution)/shard_map/while/body/eval_jaxpr/gtk,tgd->kd/dot_general | solution.py:72
  209.7 11.7 %fusion.148 = bf16[4,128,8,128]{1,3,2,0:T(8,128)(2,1)} fusion(bf16[4,128,8,128]{1,3,2,0:T(8,128)(2,1)} %get-tuple-element.250, s32[]{:T(128)} %get-tuple-element.249, f32[1664,128,8]{1,0,2:T(8,128)} %fusion.145, bf16[4,1664,128]{2,1,0:T(8,128)(2,1)} %get-tuple-element.265, f32[8,128,1664]{1,2,0:T(8,128)} %get-tuple-element.235, ...), kind=kOutput, calls=%fused_computation.26.clone.1 | convolution fusion | flops 448268928 | bytes 27960320 | tf_op jit(solution)/shard_map/while/body/eval_jaxpr/gtk,kd->tgd/dot_general | solution.py:69
  221.4 5.1 fusion.150
  227.9 6.2 %fusion.147 = (f32[8,128]{1,0:T(8,128)S(1)}, f32[8,128,1664]{1,2,0:T(8,128)}) fusion(pred[128,1664]{0,1:T(8,128)(4,1)S(1)} %fusion.146, bf16[4,1664,128]{2,1,0:T(8,128)(2,1)} %get-tuple-element.265, s32[]{:T(128)} %get-tuple-element.249, bf16[4,128,8,128]{1,3,2,0:T(8,128)(2,1)} %get-tuple-element.266), kind=kOutput, calls=%fused_computation.100.clone.1 | convolution fusion | flops 443025024 | bytes 7721984 | tf_op jit(solution)/shard_map/while/body/eval_jaxpr/sub | solution.py:63
  234.2 3.9 fusion.145
  238.0 11.7 %fusion.149 = f32[4,1664,128]{1,2,0:T(8,128)} fusion(f32[4,1664,128]{1,2,0:T(8,128)} %get-tuple-element.251, s32[]{:T(128)} %get-tuple-element.249, f32[1664,128,8]{1,0,2:T(8,128)} %fusion.145, bf16[4,128,8,128]{1,3,2,0:T(8,128)(2,1)} %get-tuple-element.266, f32[8,128,1664]{1,2,0:T(8,128)} %get-tuple-element.235, f32[8,128]{1,0:T(8,128)S(1)} %get-tuple-element.236), kind=kOutput, calls=%fused_computation.21.clone.1 | convolution fusion | flops 448137856 | bytes 28386304 | tf_op jit(solution)/shard_map/while/body/eval_jaxpr/gtk,tgd->kd/dot_general | solution.py:72
  249.7 11.7 %fusion.148 = bf16[4,128,8,128]{1,3,2,0:T(8,128)(2,1)} fusion(bf16[4,128,8,128]{1,3,2,0:T(8,128)(2,1)} %get-tuple-element.250, s32[]{:T(128)} %get-tuple-element.249, f32[1664,128,8]{1,0,2:T(8,128)} %fusion.145, bf16[4,1664,128]{2,1,0:T(8,128)(2,1)} %get-tuple-element.265, f32[8,128,1664]{1,2,0:T(8,128)} %get-tuple-element.235, ...), kind=kOutput, calls=%fused_computation.26.clone.1 | convolution fusion | flops 448268928 | bytes 27960320 | tf_op jit(solution)/shard_map/while/body/eval_jaxpr/gtk,kd->tgd/dot_general | solution.py:69
  261.4 5.1 fusion.150
  266.5 3.2 slice.74
  297.7 87.0 %all-reduce.2 = bf16[2,512,512]{2,0,1:T(2,128)(2,1)S(1)} all-reduce(f32[2,512,512]{2,0,1:T(2,128)S(1)} %copy.85), channel_id=2, replica_groups=mesh['doc'=4,'resp'=8,'prob'=4] {'doc','resp','prob'}, use_global_device_ids=true, to_apply=%region_5.6.clone | all-reduce | flops 524288 | bytes 3145728
  384.8 22.5 %all_gather.14 = bf16[2,128,512]{2,0,1:T(2,128)(2,1)S(1)} all-gather(bf16[2,4,512]{2,0,1:T(2,128)(2,1)S(1)} %dynamic-slice_convert_fusion), channel_id=1, replica_groups=mesh['doc'=4,'resp'=8,'prob'=4] {'resp','prob'}, dimensions={1}, use_global_device_ids=true | all-gather | bytes 270336 | tf_op jit(solution)/shard_map/all_gather | solution.py:87
  407.7 4.5 fusion.100
  415.1 68.6 %reduce-scatter.2.cloned.1.call-done = f32[2,32,512]{2,1,0:T(8,128)} async-done(((f32[2,1024,512]{2,1,0:T(8,128)}), f32[2,32,512]{2,1,0:T(8,128)}) %reduce-scatter.2.cloned.1.call-update) | async-done | bytes 131088 | tf_op jit(solution)/shard_map/reduce_scatter | solution.py:92
  484.6 12.3 %all_gather.15 = bf16[2,128,512]{2,1,0:T(8,128)(2,1)S(1)} all-gather(bf16[2,32,512]{2,1,0:T(8,128)(2,1)S(1)} %convert_element_type.66), channel_id=1, replica_groups=mesh['doc'=4,'resp'=8,'prob'=4] {'doc'}, dimensions={1}, use_global_device_ids=true | all-gather | bytes 327680 | tf_op jit(solution)/shard_map/all_gather | solution.py:95
  496.9 4.4 fusion.99
  (89 shorter events, 62.3 us)
Async XLA Ops:
  7.2 1.3 copy-start
  7.2 33.6 %all-gather.3.cloned.1.call-start = ((), (), s32[]{:S(2)}) async-start(), calls=%async_computation.1 | async-start | bytes 1310720 | tf_op jit(solution)/shard_map/all_gather | solution.py:32
  8.5 4.0 copy-start.3
  12.5 1.7 copy-start.4
  14.2 84.0 %all-gather.5.cloned.1.call-start = ((), (), s32[]{:S(2)}) async-start(), calls=%async_computation.2 | async-start | bytes 2359296 | tf_op jit(solution)/shard_map/all_gather | solution.py:40
  14.3 4.0 copy-start.2
  18.3 1.8 copy-start.9
  18.3 4.5 copy-start.5
  19.3 4.3 copy-start.6
  20.0 463.7 %reduce-scatter.2.cloned.1.call-start = ((), (), s32[]{:S(2)}) async-start(), calls=%async_computation.3 | async-start | bytes 4325376 | tf_op jit(solution)/shard_map/reduce_scatter | solution.py:92
  102.2 1.5 copy-start.8
  291.9 4.5 copy-start.7
  407.3 4.9 slice-start
  407.6 4.5 slice-start.1
  412.2 89.1 %slice-start.2 = ((s8[5242880]{0:T(1024)(128)(4,1)}), s8[1048576]{0:T(1024)(128)(4,1)S(1)}, s32[]{:S(2)}) async-start(s8[5242880]{0:T(1024)(128)(4,1)} %bitcast.225), calls=%async_computation.6 | async-start | bytes 2097152
  496.9 4.5 slice-start.3
  496.9 7.4 %copy-start.1 = (bf16[128,5120]{1,0:T(8,128)(2,1)S(1)}, bf16[128,5120]{1,0:T(8,128)(2,1)}, u32[]{:S(2)}) copy-start(bf16[128,5120]{1,0:T(8,128)(2,1)} %param.11) | copy-start | bytes 3932164
Sparse Core Ops, SparseCore 0:
  14.3 26.4 all-gather.2
  43.7 54.4 all-gather.4
  285.9 197.7 reduce-scatter.1
where the time goes:
time: 512 us; the launch traced here: 511 us
  matrix products  178 us (35%)
  waiting for transfers between devices  139 us (27%)
  blocking collectives  122 us (24%)
  local copies, waits for them, and re-layouts  42.5 us (8%)
  other arithmetic  15.2 us (3%)
  between operations  14.8 us (3%)
    unnamed x1, blocking collectives  87 us
    reduce_scatter x1, waiting for transfers between devices, on_device(): lax.psum_scatter(ordered, ('doc', 'resp'), scatter_dimension=1, tiled=True)  68.6 us
    all_gather x1, waiting for transfers between devices, on_device(): prompt_full = lax.all_gather(prompt_pair, 'resp', axis=1, tiled=True)  54.1 us
    dot_general x4, matrix products, per_head(): jnp.einsum('gtk,tgd->kd', dscore, qg, preferred_element_type=jnp.float32)  46.8 us
    dot_general x4, matrix products, per_head(): jnp.einsum('gtk,kd->tgd', dscore, kg, preferred_element_type=jnp.float32)  46.7 us
    sub x4, matrix products, per_head(): expo = jnp.exp(scores - peak)  24.9 us
    all_gather x1, blocking collectives, on_device(): doc_sum = lax.all_gather(doc_share, ('resp', 'prob'), axis=1, tiled=True)  22.5 us
    dot_general x4, matrix products, per_head(): jnp.einsum('gtk,tgd->kd', probs_b, gg, preferred_element_type=jnp.float32)  20.4 us
  transfers between devices with their start and end apart: 3, of which 3 were waited for; matrix products, arithmetic and copies ran while one was open for 6% of the time, Pallas kernels for 0%

commit v1 on v0

v1 whole, which is shorter than its diff:
```python
import jax
import jax.numpy as jnp
import numpy as np
from jax import lax
from jax.experimental import pallas as pl
from jax.experimental.pallas import tpu as pltpu
from jax.sharding import PartitionSpec as P

D = 5120
QH = 32
KVH = 4
HD = 128
R = 128
GROUP = QH // KVH
WIDE = GROUP * HD
KVW = 2 * HD
NZ = 4
DOC = 512
PROMPT = 1024
PRE = DOC + PROMPT
KEYS = PRE + R
SCALE = 1.0 / HD**0.5
LOG2E = 1.4426950408889634
MSG = 2 * WIDE + KVW + HD
RET = WIDE + KVW
BF = jnp.bfloat16
F32 = jnp.float32
TILE = 512
VMEM = pl.BlockSpec(memory_space=pltpu.VMEM)
SMEM = pl.BlockSpec(memory_space=pltpu.SMEM)
ANY = pl.BlockSpec(memory_space=pl.ANY)


def part(ref, start, size):
    return ref.at[:, pl.ds(pl.multiple_of(start, 128), size)]


def bundle_copies(q, cot, rk, rv, head, dst, sems, first):
    moves = [
        (part(q.at[0], head * WIDE, WIDE), dst.at[:, pl.ds(0, WIDE)]),
        (part(cot.at[0], head * WIDE, WIDE), dst.at[:, pl.ds(WIDE, WIDE)]),
        (part(rk.at[0], head * HD, HD), dst.at[:, pl.ds(2 * WIDE, HD)]),
        (part(rv.at[0], head * HD, HD), dst.at[:, pl.ds(2 * WIDE + HD, HD)]),
    ]
    return [pltpu.make_async_copy(a, b, sems.at[first + i]) for i, (a, b) in enumerate(moves)]


def live_block(length):
    rows = lax.broadcasted_iota(jnp.int32, (R, HD), 0)
    return jnp.where(rows < length, 1.0, 0.0).astype(BF)


def project_kernel(
    length, pos, xd, xp, wk, wv, q, cot, rk, rv, msg_p, msg_m, msg_2, doc0, doc2, own, acc, live, pair, sems
):
    step = pl.program_id(0)
    y = pos[0]
    heads = [lax.rem(y + 1, 4), lax.rem(y + 3, 4), lax.rem(y + 2, 4)]
    copies = []
    for i, (head, msg) in enumerate(zip(heads, (msg_p, msg_m, msg_2))):
        copies += bundle_copies(q, cot, rk, rv, head, msg, sems, 4 * i)
    for i, msg in enumerate((msg_p, msg_m, msg_2)):
        copies.append(pltpu.make_async_copy(live, msg.at[:, pl.ds(MSG - HD, HD)], sems.at[12 + i]))

    @pl.when(step == 0)
    def _():
        live[...] = live_block(length[0])
        acc[...] = jnp.zeros_like(acc)
        for c in copies:
            c.start()

    x = jnp.concatenate([xd[...], xp[0]], axis=0)
    acc[:, : KVH * HD] += jnp.dot(x, wk[...], preferred_element_type=F32)
    acc[:, KVH * HD :] += jnp.dot(x, wv[...], preferred_element_type=F32)

    @pl.when(step == pl.num_programs(0) - 1)
    def _():
        def head_pair(rows, head):
            at = pl.multiple_of(head * HD, 128)
            return jnp.concatenate(
                [acc[rows, pl.ds(at, HD)], acc[rows, pl.ds(KVH * HD + at, HD)]], axis=1
            ).astype(BF)

        doc_rows, prompt_rows = pl.ds(0, R), pl.ds(R, R)
        pair[0] = head_pair(doc_rows, heads[0])
        pair[1] = head_pair(doc_rows, heads[1])
        extra = [
            pltpu.make_async_copy(pair.at[i], msg.at[:, pl.ds(MSG, KVW)], sems.at[15 + i])
            for i, msg in enumerate((msg_p, msg_m))
        ]
        for c in extra:
            c.start()
        doc2[...] = head_pair(doc_rows, heads[2])
        doc0[...] = head_pair(doc_rows, y)
        own[...] = head_pair(prompt_rows, y)
        for c in copies + extra:
            c.wait()


def project(length, pos, x_doc, x_prompt, w_key, w_value, q, cot, rk, rv):
    out = jax.ShapeDtypeStruct
    return pl.pallas_call(
        project_kernel,
        grid=(D // TILE,),
        out_shape=(
            out((R, MSG + KVW), BF),
            out((R, MSG + KVW), BF),
            out((R, MSG), BF),
            out((R, KVW), BF),
            out((R, KVW), BF),
            out((R, KVW), BF),
        ),
        in_specs=[
            SMEM,
            SMEM,
            pl.BlockSpec((R, TILE), lambda i: (0, i)),
            pl.BlockSpec((1, R, TILE), lambda i: (0, 0, i)),
            pl.BlockSpec((TILE, KVH * HD), lambda i: (i, 0)),
            pl.BlockSpec((TILE, KVH * HD), lambda i: (i, 0)),
            ANY,
            ANY,
            ANY,
            ANY,
        ],
        out_specs=[ANY, ANY, ANY] + [pl.BlockSpec((R, KVW), lambda i: (0, 0))] * 3,
        scratch_shapes=[
            pltpu.VMEM((2 * R, 2 * KVH * HD), F32),
            pltpu.VMEM((R, HD), BF),
            pltpu.VMEM((2, R, KVW), BF),
            pltpu.SemaphoreType.DMA((17,)),
        ],
        compiler_params=pltpu.CompilerParams(vmem_limit_bytes=40 * 2**20),
        cost_estimate=pl.CostEstimate(flops=2 * 256 * D * 1024, bytes_accessed=18 * 2**20, transcendentals=0),
        name="project",
    )(length, pos, x_doc, x_prompt, w_key, w_value, q, cot, rk, rv)


CHUNKS = [(i * 256, 256) for i in range(6)] + [(PRE, R)]


def attend_one(r, msgs, kv, key_t, scores, dprobs, acc, store):
    kv[PRE:, :] = msgs[r, :, 2 * WIDE : 2 * WIDE + KVW]
    key_t[:, PRE:] = kv[PRE:, :HD].T
    live = msgs[r, :, MSG - HD : MSG] > 0
    key_row = lax.broadcasted_iota(jnp.int32, (R, R), 0)
    query_col = lax.broadcasted_iota(jnp.int32, (R, R), 1)
    allowed = (key_row <= query_col) & live
    allowed = jnp.concatenate([allowed, allowed], axis=1)
    acc[PRE:, :] = jnp.zeros((R, KVW), F32)

    def pair(j, carry):
        at = pl.multiple_of(j * KVW, 128)
        two_q = msgs[r, :, pl.ds(at, KVW)]
        two_g = msgs[r, :, pl.ds(pl.multiple_of(WIDE + j * KVW, 128), KVW)]
        nought = jnp.zeros((R, HD), BF)
        q0, q1 = two_q[:, :HD], two_q[:, HD:]
        g0 = jnp.where(live, two_g[:, :HD], nought)
        g1 = jnp.where(live, two_g[:, HD:], nought)
        q_rows = jnp.concatenate([q0, q1], axis=0)
        g_rows = jnp.concatenate([g0, g1], axis=0)
        q_t = jnp.concatenate([q0.T, q1.T], axis=1)
        g_t = jnp.concatenate([g0.T, g1.T], axis=1)
        peak = None
        for start, size in CHUNKS:
            s = jnp.dot(kv[start : start + size, :HD], q_t, preferred_element_type=F32)
            if start == PRE:
                s = jnp.where(allowed, s, -1e30)
            scores[start : start + size, :] = s
            top = jnp.max(s, axis=0, keepdims=True)
            peak = top if peak is None else jnp.maximum(peak, top)
        shift = peak * (SCALE * LOG2E)
        total = jnp.zeros((1, KVW), F32)
        delta = jnp.zeros((1, KVW), F32)
        for start, size in CHUNKS:
            rows = slice(start, start + size)
            e = jnp.exp2(scores[rows, :] * (SCALE * LOG2E) - shift)
            dp = jnp.dot(kv[rows, HD:], g_t, preferred_element_type=F32)
            total += jnp.sum(e, axis=0, keepdims=True)
            delta += jnp.sum(e * dp, axis=0, keepdims=True)
            scores[rows, :] = e
            dprobs[rows, :] = dp
        inv = 1.0 / total
        delta = delta * inv
        dq_t = jnp.zeros((HD, KVW), F32)
        for start, size in CHUNKS:
            rows = slice(start, start + size)
            p = scores[rows, :] * inv
            ds = (p * (dprobs[rows, :] - delta)).astype(BF)
            acc[rows, :HD] += jnp.dot(ds, q_rows, preferred_element_type=F32)
            acc[rows, HD:] += jnp.dot(p.astype(BF), g_rows, preferred_element_type=F32)
            dq_t += jnp.dot(key_t[:, rows], ds, preferred_element_type=F32)
        dq_t = dq_t * SCALE
        store(at, jnp.concatenate([dq_t[:, :HD].T, dq_t[:, HD:].T], axis=1).astype(BF))
        return carry

    lax.fori_loop(0, GROUP // 2, pair, 0)


def scaled(block):
    col = lax.broadcasted_iota(jnp.int32, block.shape, 1)
    return (block * jnp.where(col < HD, SCALE, 1.0)).astype(BF)


def attend_many(count, msgs, kv, key_t, scores, dprobs, acc, rets):
    key_t[:, :PRE] = kv[:PRE, :HD].T

    def response(r, carry):
        def store(at, block):
            rets[r, :, pl.ds(at, KVW)] = block

        attend_one(r, msgs, kv, key_t, scores, dprobs, acc, store)
        rets[r, :, WIDE:] = scaled(acc[PRE:, :])
        return carry

    lax.fori_loop(0, count, response, 0)


def attend_first_kernel(
    length, pos, q, cot, rk, rv, msg_m, msg_p, doc0, doc2, z0, z1, z2, z3,
    ret_0, ret_m, ret_p, kv, acc, msgs, key_t, scores, dprobs, rets, sems,
):
    copies = bundle_copies(q, cot, rk, rv, pos[0], msgs.at[0], sems, 0)
    copies += [
        pltpu.make_async_copy(msg_m, msgs.at[1], sems.at[4]),
        pltpu.make_async_copy(msg_p, msgs.at[2], sems.at[5]),
    ]
    pieces = [doc0, msg_m.at[:, pl.ds(MSG, KVW)], doc2, msg_p.at[:, pl.ds(MSG, KVW)], z0, z1, z2, z3]
    at = 0
    for i, piece in enumerate(pieces):
        rows = R if i < 4 else 2 * R
        copies.append(pltpu.make_async_copy(piece, kv.at[pl.ds(at, rows)], sems.at[6 + i]))
        at += rows
    for c in copies:
        c.start()
    acc[...] = jnp.zeros_like(acc)
    for c in copies:
        c.wait()
    msgs[0, :, MSG - HD : MSG] = live_block(length[0])
    attend_many(3, msgs, kv, key_t, scores, dprobs, acc, rets)
    outs = [
        pltpu.make_async_copy(rets.at[i], out, sems.at[i]) for i, out in enumerate((ret_0, ret_m, ret_p))
    ]
    for c in outs:
        c.start()
    for c in outs:
        c.wait()


def attend_last_kernel(
    pos, msg_2, kv_in, acc_in, ret_2, d0, d1, d2, d3, p0, p1, p2, p3,
    msgs, kv, acc, key_t, scores, dprobs, rets, sems,
):
    copies = [
        pltpu.make_async_copy(msg_2, msgs.at[0], sems.at[0]),
        pltpu.make_async_copy(kv_in, kv, sems.at[1]),
        pltpu.make_async_copy(acc_in, acc, sems.at[2]),
    ]
    for c in copies:
        c.start()
    for c in copies:
        c.wait()
    attend_many(1, msgs, kv, key_t, scores, dprobs, acc, rets)
    ret_2[...] = rets[0]
    for k, out in enumerate((d0, d1, d2, d3)):
        shard = lax.rem(pos[1] + k - pos[0] + 4, 4)
        out[...] = scaled(acc[pl.ds(pl.multiple_of(shard * R, R), R), :])
    for k, out in enumerate((p0, p1, p2, p3)):
        out[...] = scaled(acc[DOC + 2 * R * k : DOC + 2 * R * (k + 1), :])


def work_space(count, width):
    return [pltpu.VMEM((count, R, width), BF)], [
        pltpu.VMEM((HD, KEYS), BF),
        pltpu.VMEM((KEYS, KVW), F32),
        pltpu.VMEM((KEYS, KVW), F32),
        pltpu.VMEM((count, R, RET), BF),
    ]


def attend_cost(count):
    return pl.CostEstimate(
        flops=10 * count * GROUP * R * KEYS * HD * 3, bytes_accessed=2**22, transcendentals=0
    )


def attend_first(length, pos, q, cot, rk, rv, msg_m, msg_p, doc0, doc2, zs):
    out = jax.ShapeDtypeStruct
    head, tail = work_space(3, MSG + KVW)
    return pl.pallas_call(
        attend_first_kernel,
        out_shape=[out((R, RET), BF)] * 3 + [out((KEYS, KVW), BF), out((KEYS, KVW), F32)],
        in_specs=[SMEM, SMEM] + [ANY] * 12,
        out_specs=[ANY] * 3 + [VMEM] * 2,
        scratch_shapes=head + tail + [pltpu.SemaphoreType.DMA((14,))],
        compiler_params=pltpu.CompilerParams(vmem_limit_bytes=40 * 2**20),
        cost_estimate=attend_cost(3),
        name="attend_first",
    )(length, pos, q, cot, rk, rv, msg_m, msg_p, doc0, doc2, *zs)


def attend_last(pos, msg_2, kv, acc):
    out = jax.ShapeDtypeStruct
    head, tail = work_space(1, MSG)
    return pl.pallas_call(
        attend_last_kernel,
        out_shape=[out((R, RET), BF)] + [out((R, KVW), BF)] * 4 + [out((2 * R, KVW), BF)] * 4,
        in_specs=[SMEM] + [ANY] * 3,
        out_specs=[VMEM] * 9,
        scratch_shapes=head
        + [pltpu.VMEM((KEYS, KVW), BF), pltpu.VMEM((KEYS, KVW), F32)]
        + tail
        + [pltpu.SemaphoreType.DMA((3,))],
        compiler_params=pltpu.CompilerParams(vmem_limit_bytes=40 * 2**20),
        cost_estimate=attend_cost(1),
        name="attend_last",
    )(pos, msg_2, kv, acc)


def finish_kernel(
    pos, docs, prompts, wk, wv, r0, r1, r2, r3, grad_doc, grad_prompt, gq, gk, gv, left, sems
):
    step = pl.program_id(0)
    y, z = pos[0], pos[1]
    copies = []
    for k, r in enumerate((r0, r1, r2, r3)):
        head = lax.rem(y + k, 4)
        copies += [
            pltpu.make_async_copy(r.at[:, pl.ds(0, WIDE)], part(gq.at[0], head * WIDE, WIDE), sems.at[3 * k]),
            pltpu.make_async_copy(r.at[:, pl.ds(WIDE, HD)], part(gk.at[0], head * HD, HD), sems.at[3 * k + 1]),
            pltpu.make_async_copy(
                r.at[:, pl.ds(WIDE + HD, HD)], part(gv.at[0], head * HD, HD), sems.at[3 * k + 2]
            ),
        ]

    @pl.when(step == 0)
    def _():
        for c in copies:
            c.start()
        for k in range(4):
            for rows, piece, head in (
                (pl.ds(0, R), docs[k], lax.rem(z + 4 - k, 4)),
                (pl.ds(R, R), prompts[k], lax.rem(y + k, 4)),
            ):
                at = pl.multiple_of(head * HD, 128)
                left[rows, pl.ds(at, HD)] = piece[:, :HD]
                left[rows, pl.ds(KVH * HD + at, HD)] = piece[:, HD:]

    over = (((1,), (1,)), ((), ()))
    total = lax.dot_general(left[:, : KVH * HD], wk[...], over, preferred_element_type=F32)
    total += lax.dot_general(left[:, KVH * HD :], wv[...], over, preferred_element_type=F32)
    grad_doc[...] = total[:R].astype(BF)
    grad_prompt[0] = total[R:].astype(BF)

    @pl.when(step == pl.num_programs(0) - 1)
    def _():
        for c in copies:
            c.wait()


def finish(pos, docs, prompts, w_key, w_value, rets):
    out = jax.ShapeDtypeStruct
    whole = pl.BlockSpec((R, KVW), lambda i: (0, 0))
    weight = pl.BlockSpec((TILE, KVH * HD), lambda i: (i, 0))

    def body(pos, *refs):
        finish_kernel(pos, refs[:4], refs[4:8], *refs[8:])

    return pl.pallas_call(
        body,
        grid=(D // TILE,),
        out_shape=(
            out((R, D), BF),
            out((1, R, D), BF),
            out((1, R, QH * HD), BF),
            out((1, R, KVH * HD), BF),
            out((1, R, KVH * HD), BF),
        ),
        in_specs=[SMEM] + [whole] * 8 + [weight] * 2 + [ANY] * 4,
        out_specs=[
            pl.BlockSpec((R, TILE), lambda i: (0, i)),
            pl.BlockSpec((1, R, TILE), lambda i: (0, 0, i)),
            ANY,
            ANY,
            ANY,
        ],
        scratch_shapes=[pltpu.VMEM((2 * R, 2 * KVH * HD), BF), pltpu.SemaphoreType.DMA((12,))],
        compiler_params=pltpu.CompilerParams(vmem_limit_bytes=40 * 2**20),
        cost_estimate=pl.CostEstimate(flops=2 * 256 * D * 1024, bytes_accessed=18 * 2**20, transcendentals=0),
        name="finish",
    )(pos, *docs, *prompts, w_key, w_value, *rets)


def moves(axes, rule):
    sizes = [lax.axis_size(a) for a in axes]
    pairs = []
    for index in range(np.prod(sizes)):
        here = np.unravel_index(index, sizes)
        there = rule(*(int(i) for i in here))
        pairs.append((index, int(np.ravel_multi_index(there, sizes))))
    return (axes if len(axes) > 1 else axes[0]), pairs


def send(x, move):
    return lax.ppermute(x, *move)


def along_y(k):
    return moves(("doc",), lambda y: ((y + k) % 4,))


def turned(resp, k):
    return ((resp // 2 + k) % NZ) * 2 + resp % 2


def along_z(k):
    return moves(("resp",), lambda r: (turned(r, k),))


def along_x(k):
    def rule(resp, prob):
        x = ((resp % 2) * 2 + prob // 2 + k) % 4
        return (resp // 2) * 2 + x // 2, (x % 2) * 2 + prob % 2

    return moves(("resp", "prob"), rule)


def other_half():
    return moves(("resp",), lambda r: (r ^ 1,))


def other_core():
    return moves(("prob",), lambda p: (p ^ 1,))


def cross(k):
    return moves(("doc", "resp"), lambda y, r: (r // 2, ((y + k) % 4) * 2 + r % 2))


def added(*pieces):
    total = pieces[0].astype(F32)
    for piece in pieces[1:]:
        total = total + piece.astype(F32)
    return total


def on_device(x_doc, x_prompt, w_key, w_value, queries, resp_keys, resp_values, out_grad, lengths):
    y = lax.axis_index("doc")
    z = lax.axis_index("resp") // 2
    pos = jnp.stack([y, z]).astype(jnp.int32)
    msg_p, msg_m, msg_2, doc_0, doc_2, own = project(
        lengths, pos, x_doc, x_prompt, w_key, w_value, queries, out_grad, resp_keys, resp_values
    )
    half = send(own, other_half())
    msg_p = send(msg_p, along_y(1))
    msg_m = send(msg_m, along_y(-1))
    doc_2 = send(doc_2, along_y(2))
    block = jnp.concatenate([own, half], axis=0)
    blocks = [block] + [send(block, along_z(-k)) for k in (1, 2, 3)]
    msg_2 = send(msg_2, along_y(2))
    ret_0, ret_m, ret_p, kv, acc = attend_first(
        lengths, pos, queries, out_grad, resp_keys, resp_values, msg_m, msg_p, doc_0, doc_2, blocks
    )
    ret_2, *terms = attend_last(pos, msg_2, kv, acc)
    doc_terms, prompt_terms = terms[:4], terms[4:]
    doc_got = [doc_terms[0]] + [send(doc_terms[k], along_z(k)) for k in (1, 2, 3)]
    prompt_got = [prompt_terms[0]] + [send(prompt_terms[k], along_z(k)) for k in (1, 2, 3)]
    doc = added(*doc_got).astype(BF)
    doc = added(doc, send(doc, other_core())).astype(BF)
    doc = added(doc, *(send(doc, along_x(k)) for k in (1, 2, 3))).astype(BF)
    docs = [send(doc, cross(k)) for k in range(4)]
    prompt = added(*prompt_got)
    prompt = (prompt[:R] + send(prompt[R:].astype(BF), other_half()).astype(F32)).astype(BF)
    prompts = [prompt] + [send(prompt, along_y(-k)) for k in (1, 2, 3)]
    rets = [ret_0, send(ret_p, along_y(-1)), send(ret_2, along_y(2)), send(ret_m, along_y(1))]
    grad_doc, grad_prompt, gq, gk, gv = finish(pos, docs, prompts, w_key, w_value, rets)
    return gq, gk, gv, grad_doc, grad_prompt


def solution(mesh):
    placed = (
        P("doc", None),
        P("prob", "resp", None),
        P(),
        P(),
        P(("doc", "resp", "prob"), None, None),
        P(("doc", "resp", "prob"), None, None),
        P(("doc", "resp", "prob"), None, None),
        P(("doc", "resp", "prob"), None, None),
        P(("doc", "resp", "prob")),
    )
    return jax.shard_map(
        on_device,
        mesh=mesh,
        in_specs=placed,
        out_specs=(
            P(("doc", "resp", "prob"), None, None),
            P(("doc", "resp", "prob"), None, None),
            P(("doc", "resp", "prob"), None, None),
            P("doc", None),
            P("prob", "resp", None),
        ),
        check_vma=False,
    )
```

time: 512 us -> 156 us (0.30)
  matrix products: 178 us -> 0 us
  blocking collectives: 122 us -> 0 us
  waiting for transfers between devices: 139 us -> 37.6 us
  Pallas kernels: 0 us -> 54 us
  starting transfers between devices: 0.12 us -> 52.6 us
  local copies, waits for them, and re-layouts: 42.5 us -> 9.43 us
  other arithmetic: 15.2 us -> 0.25 us
  between operations: 14.8 us -> 1.67 us
    dot_general x24 -> x0, matrix products: 153 us -> none  [the longest x4 46.8 us: per_head(): jnp.einsum('gtk,tgd->kd', dscore, qg, preferred_element_type=jnp.float32)]
    unnamed x1 -> x0, blocking collectives: 87 us -> none
    all_gather x2 -> x0, waiting for transfers between devices: 70 us -> none  [the longest x1 54.1 us: on_device(): prompt_full = lax.all_gather(prompt_pair, 'resp', axis=1, tiled=True)]
    reduce_scatter x1 -> x0, waiting for transfers between devices: 68.6 us -> none  [on_device(): lax.psum_scatter(ordered, ('doc', 'resp'), scatter_dimension=1, tiled=True)]
    pallas_call x0 -> x4, Pallas kernels: none -> 54 us  [the longest x1 28 us: attend_first(): pl.pallas_call(attend_first_kernel, out_shape=[out((R, RET), BF)] * 3 + [...]
    ppermute x0 -> x29, starting transfers between devices: none -> 52.6 us  [send(): return lax.ppermute(x, *move)]
    ppermute x0 -> x29, waiting for transfers between devices: none -> 37.6 us  [send(): return lax.ppermute(x, *move)]
    all_gather x2 -> x0, blocking collectives: 34.7 us -> none  [the longest x1 22.5 us: on_device(): doc_sum = lax.all_gather(doc_share, ('resp', 'prob'), axis=1, tiled=True)]
  transfers between devices with their start and end apart: 3 -> 29, of which waited for: 3 -> 13; matrix products, arithmetic and copies ran while one was open for 6% -> 0% of each run, Pallas kernels for 0% -> 18%
where the time goes in v1:
time: 156 us; the launch traced here: 155 us
  Pallas kernels  54 us (35%)
  starting transfers between devices  52.6 us (34%)
  waiting for transfers between devices  37.6 us (24%)
  local copies, waits for them, and re-layouts  9.43 us (6%)
  between operations  1.67 us (1%)
    ppermute x29, starting transfers between devices, send(): return lax.ppermute(x, *move)  52.6 us
    ppermute x29, waiting for transfers between devices, send(): return lax.ppermute(x, *move)  37.6 us
    pallas_call x1, Pallas kernels, attend_first(): pl.pallas_call(attend_first_kernel, out_shape=[out((R, RET), BF)] * 3 + [...  28 us
    pallas_call x1, Pallas kernels, attend_last(): pl.pallas_call(attend_last_kernel, out_shape=[out((R, RET), BF)] + [out((...  9.61 us
    unnamed x29, local copies, waits for them, and re-layouts  9.41 us
    pallas_call x1, Pallas kernels, project(): pl.pallas_call(project_kernel, grid=(D // TILE,), out_shape=(out((R, MSG...  9.02 us
    pallas_call x1, Pallas kernels, finish(): pl.pallas_call(body, grid=(D // TILE,), out_shape=(out((R, D), BF), out((...  7.42 us
  transfers between devices with their start and end apart: 29, of which 13 were waited for; matrix products, arithmetic and copies ran while one was open for 0% of the time, Pallas kernels for 18%

profile of v1, /device:TPU:0, one launch (start us, length us, event | category | flops | bytes accessed | tf_op | source)
XLA Modules:
  0.0 155.5 jit_solution(5701367456977247061)
XLA Ops:
  1.4 2.5 %copy-done = bf16[5120,512]{1,0:T(8,128)(2,1)S(1)} copy-done((bf16[5120,512]{1,0:T(8,128)(2,1)S(1)}, bf16[5120,512]{1,0:T(8,128)(2,1)}, u32[]{:S(2)}) %copy-start) | copy-done | bytes 5242904
  3.9 1.3 copy-done.1
  10.8 9.0 %project.1 = (bf16[128,2688]{1,0:T(8,128)(2,1)S(1)}, bf16[128,2688]{1,0:T(8,128)(2,1)S(1)}, bf16[128,2432]{1,0:T(8,128)(2,1)S(1)}, bf16[128,256]{1,0:T(8,128)(2,...) custom-call(s32[1]{0:T(128)S(6)} %copy.15.length, s32[2]{0:T(128)S(1)} %pad_add_fusion.pos, ...), custom_call_target="tpu_custom_call" | custom-call | flops 2684354560 | bytes 18874368 | tf_op jit(solution)/shard_map/project/pallas_call | solution.py:102
  19.8 3.2 %collective-permute-start.1 = (bf16[128,2688]{1,0:T(8,128)(2,1)S(1)}, bf16[128,2688]{1,0:T(8,128)(2,1)S(1)}, u32[]{:S(2)}, u32[]{:S(2)}) collective-permute-start(bf16[128,2688]{1,0:T(8,128)(2,1)S(1)} %get-tuple-element.31), channel_id=1, source_target_pairs={{0,96},{32,0},{64,32},{96,64},{1,97},{33,1},{65,33},{97,65},{2,98}... | collective-permute-start | bytes 2064392 | tf_op jit(solution)/shard_map/ppermute | solution.py:404
  22.9 2.2 %collective-permute-start.3 = (bf16[128,256]{1,0:T(8,128)(2,1)S(1)}, bf16[128,256]{1,0:T(8,128)(2,1)S(1)}, u32[]{:S(2)}, u32[]{:S(2)}) collective-permute-start(bf16[128,256]{1,0:T(8,128)(2,1)S(1)} %get-tuple-element.34), channel_id=1, source_target_pairs={{0,64},{32,96},{64,0},{96,32},{1,65},{33,97},{65,1},{97,33},{2,66}... | collective-permute-start | bytes 196616 | tf_op jit(solution)/shard_map/ppermute | solution.py:404
  25.2 3.0 %collective-permute-start.4 = (bf16[128,256]{1,0:T(8,128)(2,1)S(1)}, bf16[128,256]{1,0:T(8,128)(2,1)S(1)}, u32[]{:S(2)}, u32[]{:S(2)}) collective-permute-start(bf16[128,256]{1,0:T(8,128)(2,1)S(1)} %get-tuple-element.35), channel_id=1, source_target_pairs={{0,4},{4,0},{8,12},{12,8},{16,20},{20,16},{24,28},{28,24},{1,5},{5... | collective-permute-start | bytes 196616 | tf_op jit(solution)/shard_map/ppermute | solution.py:404
  28.2 2.7 %collective-permute-done.4 = bf16[128,256]{1,0:T(8,128)(2,1)S(1)} collective-permute-done((bf16[128,256]{1,0:T(8,128)(2,1)S(1)}, bf16[128,256]{1,0:T(8,128)(2,1)S(1)}, u32[]{:S(2)}, u32[]{:S(2)}) %collective-permute-start.4) | collective-permute-done | bytes 65568 | tf_op jit(solution)/shard_map/ppermute | solution.py:404
  30.9 1.9 %collective-permute-start.7 = (bf16[256,256]{1,0:T(8,128)(2,1)S(1)}, bf16[256,256]{1,0:T(8,128)(2,1)S(1)}, u32[]{:S(2)}, u32[]{:S(2)}) collective-permute-start(bf16[256,256]{1,0:T(8,128)(2,1)S(1)} %constant_dynamic-update-slice_fusion.z0), channel_id=1, source_target_pairs={{0,8},{4,12},{8,16},{12,20},{16,24},{20,28},{24,0},{28,4},{1,9},{5... | collective-permute-start | bytes 393224 | tf_op jit(solution)/shard_map/ppermute | solution.py:404
  32.8 3.6 %collective-permute-start.6 = (bf16[256,256]{1,0:T(8,128)(2,1)S(1)}, bf16[256,256]{1,0:T(8,128)(2,1)S(1)}, u32[]{:S(2)}, u32[]{:S(2)}) collective-permute-start(bf16[256,256]{1,0:T(8,128)(2,1)S(1)} %constant_dynamic-update-slice_fusion.z0), channel_id=1, source_target_pairs={{0,16},{4,20},{8,24},{12,28},{16,0},{20,4},{24,8},{28,12},{1,17},{... | collective-permute-start | bytes 393224 | tf_op jit(solution)/shard_map/ppermute | solution.py:404
  36.4 5.1 %collective-permute-done.3.doc2 = bf16[128,256]{1,0:T(8,128)(2,1)S(1)} collective-permute-done((bf16[128,256]{1,0:T(8,128)(2,1)S(1)}, bf16[128,256]{1,0:T(8,128)(2,1)S(1)}, u32[]{:S(2)}, u32[]{:S(2)}) %collective-permute-start.3) | collective-permute-done | bytes 65568 | tf_op jit(solution)/shard_map/ppermute | solution.py:404
  41.5 4.0 %collective-permute-start.5 = (bf16[256,256]{1,0:T(8,128)(2,1)S(1)}, bf16[256,256]{1,0:T(8,128)(2,1)S(1)}, u32[]{:S(2)}, u32[]{:S(2)}) collective-permute-start(bf16[256,256]{1,0:T(8,128)(2,1)S(1)} %constant_dynamic-update-slice_fusion.z0), channel_id=1, source_target_pairs={{0,24},{4,28},{8,0},{12,4},{16,8},{20,12},{24,16},{28,20},{1,25},{... | collective-permute-start | bytes 393224 | tf_op jit(solution)/shard_map/ppermute | solution.py:404
  45.6 1.5 collective-permute-start
  48.1 28.0 %attend_first.1 = (bf16[128,1280]{1,0:T(8,128)(2,1)S(1)}, bf16[128,1280]{1,0:T(8,128)(2,1)S(1)}, bf16[128,1280]{1,0:T(8,128)(2,1)S(1)}, bf16[1664,256]{1,0:T(8,128)(2,1)S(1)}, f32[1664,256]{1,0:T(8,128)S(1)}) custom-call(s32[1]{0:T(128)S(6)} %copy.15.length, s32[2]{0:T(128)S(1)} %pad_add_fusion.pos, bf16[1,128,4096]{2,1,0:T(8,128)(2,1)S(1)} %copy-done.4, ...), custom_call_target="tpu_custom_call" | custom-call | flops 19629342720 | bytes 4194304 | tf_op jit(solution)/shard_map/attend_first/pallas_call | solution.py:289
  76.2 9.6 %attend_last.1 = (bf16[128,1280]{1,0:T(8,128)(2,1)S(1)}, bf16[128,256]{1,0:T(8,128)(2,1)S(1)}, bf16[128,256]{1,0:T(8,128)(2,1)S(1)}, bf16[128,256]{1,0:T(8,128)(...) custom-call(s32[2]{0:T(128)S(1)} %pad_add_fusion.pos, ...), custom_call_target="tpu_custom_call" | custom-call | flops 6543114240 | bytes 4194304 | tf_op jit(solution)/shard_map/attend_last/pallas_call | solution.py:304
  86.2 4.8 %collective-permute-start.9 = (bf16[128,256]{1,0:T(8,128)(2,1)S(1)}, bf16[128,256]{1,0:T(8,128)(2,1)S(1)}, u32[]{:S(2)}, u32[]{:S(2)}) collective-permute-start(bf16[128,256]{1,0:T(8,128)(2,1)S(1)} %get-tuple-element.40), channel_id=1, source_target_pairs={{0,16},{4,20},{8,24},{12,28},{16,0},{20,4},{24,8},{28,12},{1,17},{... | collective-permute-start | bytes 196616 | tf_op jit(solution)/shard_map/ppermute | solution.py:404
  91.7 2.2 %collective-permute-done.9 = bf16[128,256]{1,0:T(8,128)(2,1)S(1)} collective-permute-done((bf16[128,256]{1,0:T(8,128)(2,1)S(1)}, bf16[128,256]{1,0:T(8,128)(2,1)S(1)}, u32[]{:S(2)}, u32[]{:S(2)}) %collective-permute-start.9) | collective-permute-done | bytes 65568 | tf_op jit(solution)/shard_map/ppermute | solution.py:404
  93.9 1.3 collective-permute-done.10
  95.4 2.7 %collective-permute-start.20 = (bf16[256,256]{1,0:T(8,128)(2,1)S(1)}, bf16[256,256]{1,0:T(8,128)(2,1)S(1)}, u32[]{:S(2)}, u32[]{:S(2)}) collective-permute-start(bf16[256,256]{1,0:T(8,128)(2,1)S(1)} %get-tuple-element.44), channel_id=1, source_target_pairs={{0,16},{4,20},{8,24},{12,28},{16,0},{20,4},{24,8},{28,12},{1,17},{... | collective-permute-start | bytes 393224 | tf_op jit(solution)/shard_map/ppermute | solution.py:404
  98.1 1.5 collective-permute-start.21
  99.6 2.8 %collective-permute-start.14 = (bf16[128,256]{1,0:T(8,128)(2,1)S(1)}, bf16[128,256]{1,0:T(8,128)(2,1)S(1)}, u32[]{:S(2)}, u32[]{:S(2)}) collective-permute-start(bf16[128,256]{1,0:T(8,128)(2,1)S(1)} %add_convert_fusion.1), channel_id=1, source_target_pairs={{0,6},{1,7},{2,0},{3,1},{4,2},{5,3},{6,4},{7,5},{8,14},{9,15},{10,... | collective-permute-start | bytes 196616 | tf_op jit(solution)/shard_map/ppermute | solution.py:404
  103.2 2.1 %collective-permute-done.19 = bf16[256,256]{1,0:T(8,128)(2,1)S(1)} collective-permute-done((bf16[256,256]{1,0:T(8,128)(2,1)S(1)}, bf16[256,256]{1,0:T(8,128)(2,1)S(1)}, u32[]{:S(2)}, u32[]{:S(2)}) %collective-permute-start.19) | collective-permute-done | bytes 131104 | tf_op jit(solution)/shard_map/ppermute | solution.py:404
  105.3 1.5 collective-permute-start.12
  106.9 3.0 %collective-permute-start.22 = (bf16[128,256]{1,0:T(8,128)(2,1)S(1)}, bf16[128,256]{1,0:T(8,128)(2,1)S(1)}, u32[]{:S(2)}, u32[]{:S(2)}) collective-permute-start(bf16[128,256]{1,0:T(8,128)(2,1)S(1)} %slice.15), channel_id=1, source_target_pairs={{0,4},{4,0},{8,12},{12,8},{16,20},{20,16},{24,28},{28,24},{1,5},{5... | collective-permute-start | bytes 196616 | tf_op jit(solution)/shard_map/ppermute | solution.py:404
  113.2 2.6 %collective-permute-start.26 = (bf16[128,1280]{1,0:T(8,128)(2,1)S(1)}, bf16[128,1280]{1,0:T(8,128)(2,1)S(1)}, u32[]{:S(2)}, u32[]{:S(2)}) collective-permute-start(bf16[128,1280]{1,0:T(8,128)(2,1)S(1)} %get-tuple-element.47), channel_id=1, source_target_pairs={{0,96},{32,0},{64,32},{96,64},{1,97},{33,1},{65,33},{97,65},{2,98}... | collective-permute-start | bytes 983048 | tf_op jit(solution)/shard_map/ppermute | solution.py:404
  115.9 2.4 %collective-permute-start.17 = (bf16[128,256]{1,0:T(8,128)(2,1)S(1)}, bf16[128,256]{1,0:T(8,128)(2,1)S(1)}, u32[]{:S(2)}, u32[]{:S(2)}) collective-permute-start(bf16[128,256]{1,0:T(8,128)(2,1)S(1)} %add_convert_fusion), channel_id=1, source_target_pairs={{0,16},{4,20},{8,48},{12,52},{16,80},{20,84},{24,112},{28,116},{32... | collective-permute-start | bytes 196616 | tf_op jit(solution)/shard_map/ppermute | solution.py:404
  118.3 13.5 %collective-permute-done.17.refs_2_ = bf16[128,256]{1,0:T(8,128)(2,1)S(1)} collective-permute-done((bf16[128,256]{1,0:T(8,128)(2,1)S(1)}, bf16[128,256]{1,0:T(8,128)(2,1)S(1)}, u32[]{:S(2)}, u32[]{:S(2)}) %collective-permute-start.17) | collective-permute-done | bytes 65568 | tf_op jit(solution)/shard_map/ppermute | solution.py:404
  132.5 4.0 %collective-permute-done.16.refs_1_ = bf16[128,256]{1,0:T(8,128)(2,1)S(1)} collective-permute-done((bf16[128,256]{1,0:T(8,128)(2,1)S(1)}, bf16[128,256]{1,0:T(8,128)(2,1)S(1)}, u32[]{:S(2)}, u32[]{:S(2)}) %collective-permute-start.16) | collective-permute-done | bytes 65568 | tf_op jit(solution)/shard_map/ppermute | solution.py:404
  136.5 3.4 %collective-permute-start.25 = (bf16[128,256]{1,0:T(8,128)(2,1)S(1)}, bf16[128,256]{1,0:T(8,128)(2,1)S(1)}, u32[]{:S(2)}, u32[]{:S(2)}) collective-permute-start(bf16[128,256]{1,0:T(8,128)(2,1)S(1)} %fusion.refs_4_), channel_id=1, source_target_pairs={{0,32},{32,64},{64,96},{96,0},{1,33},{33,65},{65,97},{97,1},{2,34}... | collective-permute-start | bytes 196616 | tf_op jit(solution)/shard_map/ppermute | solution.py:404
  139.9 1.6 %collective-permute-start.24 = (bf16[128,256]{1,0:T(8,128)(2,1)S(1)}, bf16[128,256]{1,0:T(8,128)(2,1)S(1)}, u32[]{:S(2)}, u32[]{:S(2)}) collective-permute-start(bf16[128,256]{1,0:T(8,128)(2,1)S(1)} %fusion.refs_4_), channel_id=1, source_target_pairs={{0,64},{32,96},{64,0},{96,32},{1,65},{33,97},{65,1},{97,33},{2,66}... | collective-permute-start | bytes 196616 | tf_op jit(solution)/shard_map/ppermute | solution.py:404
  142.0 2.7 %collective-permute-start.23 = (bf16[128,256]{1,0:T(8,128)(2,1)S(1)}, bf16[128,256]{1,0:T(8,128)(2,1)S(1)}, u32[]{:S(2)}, u32[]{:S(2)}) collective-permute-start(bf16[128,256]{1,0:T(8,128)(2,1)S(1)} %fusion.refs_4_), channel_id=1, source_target_pairs={{0,96},{32,0},{64,32},{96,64},{1,97},{33,1},{65,33},{97,65},{2,98}... | collective-permute-start | bytes 196616 | tf_op jit(solution)/shard_map/ppermute | solution.py:404
  145.7 2.1 %collective-permute-done.23.refs_5_ = bf16[128,256]{1,0:T(8,128)(2,1)S(1)} collective-permute-done((bf16[128,256]{1,0:T(8,128)(2,1)S(1)}, bf16[128,256]{1,0:T(8,128)(2,1)S(1)}, u32[]{:S(2)}, u32[]{:S(2)}) %collective-permute-start.23) | collective-permute-done | bytes 65568 | tf_op jit(solution)/shard_map/ppermute | solution.py:404
  147.9 7.4 %finish.1 = (bf16[128,5120]{1,0:T(8,128)(2,1)}, bf16[1,128,5120]{2,1,0:T(8,128)(2,1)}, bf16[1,128,4096]{2,1,0:T(8,128)(2,1)}, bf16[1,128,512]{2,1,0:T(8,128)(2,1)}, bf16[1,128,512]{2,1,0:T(8,128)(2,1)}) custom-call(s32[2]{0:T(128)S(1)} %pad_add_fusion.pos, bf16[128,256]{1,0:T(8,128)(2,1)S(1)} %collective-permute-done.15.refs_0_, ...), custom_call_target="tpu_custom_call" | custom-call | flops 2684354560 | bytes 18874368 | tf_op jit(solution)/shard_map/finish/pallas_call | solution.py:368
  (69 shorter events, 14.5 us)
Async XLA Ops:
  19.8 28.3 %collective-permute-start.1 = (bf16[128,2688]{1,0:T(8,128)(2,1)S(1)}, bf16[128,2688]{1,0:T(8,128)(2,1)S(1)}, u32[]{:S(2)}, u32[]{:S(2)}) collective-permute-start(bf16[128,2688]{1,0:T(8,128)(2,1)S(1)} %get-tuple-element.31), channel_id=1, source_target_pairs={{0,96},{32,0},{64,32},{96,64},{1,97},{33,1},{65,33},{97,65},{2,98}... | collective-permute-start | bytes 2064392 | tf_op jit(solution)/shard_map/ppermute | solution.py:404
  22.9 25.2 %collective-permute-start.2 = (bf16[128,2688]{1,0:T(8,128)(2,1)S(1)}, bf16[128,2688]{1,0:T(8,128)(2,1)S(1)}, u32[]{:S(2)}, u32[]{:S(2)}) collective-permute-start(bf16[128,2688]{1,0:T(8,128)(2,1)S(1)} %get-tuple-element.32), channel_id=1, source_target_pairs={{0,32},{32,64},{64,96},{96,0},{1,33},{33,65},{65,97},{97,1},{2,34}... | collective-permute-start | bytes 2064392 | tf_op jit(solution)/shard_map/ppermute | solution.py:404
  22.9 18.6 %collective-permute-start.3 = (bf16[128,256]{1,0:T(8,128)(2,1)S(1)}, bf16[128,256]{1,0:T(8,128)(2,1)S(1)}, u32[]{:S(2)}, u32[]{:S(2)}) collective-permute-start(bf16[128,256]{1,0:T(8,128)(2,1)S(1)} %get-tuple-element.34), channel_id=1, source_target_pairs={{0,64},{32,96},{64,0},{96,32},{1,65},{33,97},{65,1},{97,33},{2,66}... | collective-permute-start | bytes 196616 | tf_op jit(solution)/shard_map/ppermute | solution.py:404
  25.2 5.8 %collective-permute-start.4 = (bf16[128,256]{1,0:T(8,128)(2,1)S(1)}, bf16[128,256]{1,0:T(8,128)(2,1)S(1)}, u32[]{:S(2)}, u32[]{:S(2)}) collective-permute-start(bf16[128,256]{1,0:T(8,128)(2,1)S(1)} %get-tuple-element.35), channel_id=1, source_target_pairs={{0,4},{4,0},{8,12},{12,8},{16,20},{20,16},{24,28},{28,24},{1,5},{5... | collective-permute-start | bytes 196616 | tf_op jit(solution)/shard_map/ppermute | solution.py:404
  30.9 14.6 %collective-permute-start.7 = (bf16[256,256]{1,0:T(8,128)(2,1)S(1)}, bf16[256,256]{1,0:T(8,128)(2,1)S(1)}, u32[]{:S(2)}, u32[]{:S(2)}) collective-permute-start(bf16[256,256]{1,0:T(8,128)(2,1)S(1)} %constant_dynamic-update-slice_fusion.z0), channel_id=1, source_target_pairs={{0,8},{4,12},{8,16},{12,20},{16,24},{20,28},{24,0},{28,4},{1,9},{5... | collective-permute-start | bytes 393224 | tf_op jit(solution)/shard_map/ppermute | solution.py:404
  32.8 14.2 %collective-permute-start.6 = (bf16[256,256]{1,0:T(8,128)(2,1)S(1)}, bf16[256,256]{1,0:T(8,128)(2,1)S(1)}, u32[]{:S(2)}, u32[]{:S(2)}) collective-permute-start(bf16[256,256]{1,0:T(8,128)(2,1)S(1)} %constant_dynamic-update-slice_fusion.z0), channel_id=1, source_target_pairs={{0,16},{4,20},{8,24},{12,28},{16,0},{20,4},{24,8},{28,12},{1,17},{... | collective-permute-start | bytes 393224 | tf_op jit(solution)/shard_map/ppermute | solution.py:404
  41.5 6.6 %collective-permute-start.5 = (bf16[256,256]{1,0:T(8,128)(2,1)S(1)}, bf16[256,256]{1,0:T(8,128)(2,1)S(1)}, u32[]{:S(2)}, u32[]{:S(2)}) collective-permute-start(bf16[256,256]{1,0:T(8,128)(2,1)S(1)} %constant_dynamic-update-slice_fusion.z0), channel_id=1, source_target_pairs={{0,24},{4,28},{8,0},{12,4},{16,8},{20,12},{24,16},{28,20},{1,25},{... | collective-permute-start | bytes 393224 | tf_op jit(solution)/shard_map/ppermute | solution.py:404
  45.6 30.5 %collective-permute-start = (bf16[128,2432]{1,0:T(8,128)(2,1)S(1)}, bf16[128,2432]{1,0:T(8,128)(2,1)S(1)}, u32[]{:S(2)}, u32[]{:S(2)}) collective-permute-start(bf16[128,2432]{1,0:T(8,128)(2,1)S(1)} %get-tuple-element.30), channel_id=1, source_target_pairs={{0,64},{32,96},{64,0},{96,32},{1,65},{33,97},{65,1},{97,33},{2,66}... | collective-permute-start | bytes 1867784 | tf_op jit(solution)/shard_map/ppermute | solution.py:404
  76.1 71.7 %slice-start = ((s8[5242880]{0:T(1024)(128)(4,1)}), s8[4194304]{0:T(1024)(128)(4,1)S(1)}, s32[]{:S(2)}) async-start(s8[5242880]{0:T(1024)(128)(4,1)} %bitcast.2), calls=%async_computation | async-start | bytes 8388608
  76.1 71.7 %slice-start.2 = ((s8[5242880]{0:T(1024)(128)(4,1)}), s8[4194304]{0:T(1024)(128)(4,1)S(1)}, s32[]{:S(2)}) async-start(s8[5242880]{0:T(1024)(128)(4,1)} %bitcast.4), calls=%async_computation.2 | async-start | bytes 8388608
  76.1 71.7 %slice-start.1 = ((s8[5242880]{0:T(1024)(128)(4,1)}), s8[1048576]{0:T(1024)(128)(4,1)S(1)}, s32[]{:S(2)}) async-start(s8[5242880]{0:T(1024)(128)(4,1)} %bitcast.2), calls=%async_computation.1 | async-start | bytes 2097152
  85.8 6.0 %collective-permute-start.8 = (bf16[128,256]{1,0:T(8,128)(2,1)S(1)}, bf16[128,256]{1,0:T(8,128)(2,1)S(1)}, u32[]{:S(2)}, u32[]{:S(2)}) collective-permute-start(bf16[128,256]{1,0:T(8,128)(2,1)S(1)} %get-tuple-element.39), channel_id=1, source_target_pairs={{0,8},{4,12},{8,16},{12,20},{16,24},{20,28},{24,0},{28,4},{1,9},{5... | collective-permute-start | bytes 196616 | tf_op jit(solution)/shard_map/ppermute | solution.py:404
  86.2 7.7 %collective-permute-start.9 = (bf16[128,256]{1,0:T(8,128)(2,1)S(1)}, bf16[128,256]{1,0:T(8,128)(2,1)S(1)}, u32[]{:S(2)}, u32[]{:S(2)}) collective-permute-start(bf16[128,256]{1,0:T(8,128)(2,1)S(1)} %get-tuple-element.40), channel_id=1, source_target_pairs={{0,16},{4,20},{8,24},{12,28},{16,0},{20,4},{24,8},{28,12},{1,17},{... | collective-permute-start | bytes 196616 | tf_op jit(solution)/shard_map/ppermute | solution.py:404
  91.0 4.3 %collective-permute-start.10 = (bf16[128,256]{1,0:T(8,128)(2,1)S(1)}, bf16[128,256]{1,0:T(8,128)(2,1)S(1)}, u32[]{:S(2)}, u32[]{:S(2)}) collective-permute-start(bf16[128,256]{1,0:T(8,128)(2,1)S(1)} %get-tuple-element.41), channel_id=1, source_target_pairs={{0,24},{4,28},{8,0},{12,4},{16,8},{20,12},{24,16},{28,20},{1,25},{... | collective-permute-start | bytes 196616 | tf_op jit(solution)/shard_map/ppermute | solution.py:404
  95.3 4.3 %collective-permute-start.11 = (bf16[128,256]{1,0:T(8,128)(2,1)S(1)}, bf16[128,256]{1,0:T(8,128)(2,1)S(1)}, u32[]{:S(2)}, u32[]{:S(2)}) collective-permute-start(bf16[128,256]{1,0:T(8,128)(2,1)S(1)} %add_convert_fusion.2), channel_id=1, source_target_pairs={{0,1},{1,0},{2,3},{3,2},{4,5},{5,4},{6,7},{7,6},{8,9},{9,8},{10,11... | collective-permute-start | bytes 196616 | tf_op jit(solution)/shard_map/ppermute | solution.py:404
  95.4 9.9 %collective-permute-start.19 = (bf16[256,256]{1,0:T(8,128)(2,1)S(1)}, bf16[256,256]{1,0:T(8,128)(2,1)S(1)}, u32[]{:S(2)}, u32[]{:S(2)}) collective-permute-start(bf16[256,256]{1,0:T(8,128)(2,1)S(1)} %get-tuple-element.43), channel_id=1, source_target_pairs={{0,8},{4,12},{8,16},{12,20},{16,24},{20,28},{24,0},{28,4},{1,9},{5... | collective-permute-start | bytes 393224 | tf_op jit(solution)/shard_map/ppermute | solution.py:404
  95.4 11.3 %collective-permute-start.20 = (bf16[256,256]{1,0:T(8,128)(2,1)S(1)}, bf16[256,256]{1,0:T(8,128)(2,1)S(1)}, u32[]{:S(2)}, u32[]{:S(2)}) collective-permute-start(bf16[256,256]{1,0:T(8,128)(2,1)S(1)} %get-tuple-element.44), channel_id=1, source_target_pairs={{0,16},{4,20},{8,24},{12,28},{16,0},{20,4},{24,8},{28,12},{1,17},{... | collective-permute-start | bytes 393224 | tf_op jit(solution)/shard_map/ppermute | solution.py:404
  98.1 8.7 %collective-permute-start.21 = (bf16[256,256]{1,0:T(8,128)(2,1)S(1)}, bf16[256,256]{1,0:T(8,128)(2,1)S(1)}, u32[]{:S(2)}, u32[]{:S(2)}) collective-permute-start(bf16[256,256]{1,0:T(8,128)(2,1)S(1)} %get-tuple-element.45), channel_id=1, source_target_pairs={{0,24},{4,28},{8,0},{12,4},{16,8},{20,12},{24,16},{28,20},{1,25},{... | collective-permute-start | bytes 393224 | tf_op jit(solution)/shard_map/ppermute | solution.py:404
  99.6 10.3 %collective-permute-start.14 = (bf16[128,256]{1,0:T(8,128)(2,1)S(1)}, bf16[128,256]{1,0:T(8,128)(2,1)S(1)}, u32[]{:S(2)}, u32[]{:S(2)}) collective-permute-start(bf16[128,256]{1,0:T(8,128)(2,1)S(1)} %add_convert_fusion.1), channel_id=1, source_target_pairs={{0,6},{1,7},{2,0},{3,1},{4,2},{5,3},{6,4},{7,5},{8,14},{9,15},{10,... | collective-permute-start | bytes 196616 | tf_op jit(solution)/shard_map/ppermute | solution.py:404
  102.4 7.4 %collective-permute-start.13 = (bf16[128,256]{1,0:T(8,128)(2,1)S(1)}, bf16[128,256]{1,0:T(8,128)(2,1)S(1)}, u32[]{:S(2)}, u32[]{:S(2)}) collective-permute-start(bf16[128,256]{1,0:T(8,128)(2,1)S(1)} %add_convert_fusion.1), channel_id=1, source_target_pairs={{0,4},{1,5},{2,6},{3,7},{4,0},{5,1},{6,2},{7,3},{8,12},{9,13},{10,... | collective-permute-start | bytes 196616 | tf_op jit(solution)/shard_map/ppermute | solution.py:404
  105.3 5.8 %collective-permute-start.12 = (bf16[128,256]{1,0:T(8,128)(2,1)S(1)}, bf16[128,256]{1,0:T(8,128)(2,1)S(1)}, u32[]{:S(2)}, u32[]{:S(2)}) collective-permute-start(bf16[128,256]{1,0:T(8,128)(2,1)S(1)} %add_convert_fusion.1), channel_id=1, source_target_pairs={{0,2},{1,3},{2,4},{3,5},{4,6},{5,7},{6,0},{7,1},{8,10},{9,11},{10,... | collective-permute-start | bytes 196616 | tf_op jit(solution)/shard_map/ppermute | solution.py:404
  106.9 9.0 %collective-permute-start.22 = (bf16[128,256]{1,0:T(8,128)(2,1)S(1)}, bf16[128,256]{1,0:T(8,128)(2,1)S(1)}, u32[]{:S(2)}, u32[]{:S(2)}) collective-permute-start(bf16[128,256]{1,0:T(8,128)(2,1)S(1)} %slice.15), channel_id=1, source_target_pairs={{0,4},{4,0},{8,12},{12,8},{16,20},{20,16},{24,28},{28,24},{1,5},{5... | collective-permute-start | bytes 196616 | tf_op jit(solution)/shard_map/ppermute | solution.py:404
  111.1 7.2 %collective-permute-start.18 = (bf16[128,256]{1,0:T(8,128)(2,1)S(1)}, bf16[128,256]{1,0:T(8,128)(2,1)S(1)}, u32[]{:S(2)}, u32[]{:S(2)}) collective-permute-start(bf16[128,256]{1,0:T(8,128)(2,1)S(1)} %add_convert_fusion), channel_id=1, source_target_pairs={{0,24},{4,28},{8,56},{12,60},{16,88},{20,92},{24,120},{28,124},{32... | collective-permute-start | bytes 196616 | tf_op jit(solution)/shard_map/ppermute | solution.py:404
  112.0 35.8 %collective-permute-start.27 = (bf16[128,1280]{1,0:T(8,128)(2,1)S(1)}, bf16[128,1280]{1,0:T(8,128)(2,1)S(1)}, u32[]{:S(2)}, u32[]{:S(2)}) collective-permute-start(bf16[128,1280]{1,0:T(8,128)(2,1)S(1)} %get-tuple-element.48), channel_id=1, source_target_pairs={{0,64},{32,96},{64,0},{96,32},{1,65},{33,97},{65,1},{97,33},{2,66}... | collective-permute-start | bytes 983048 | tf_op jit(solution)/shard_map/ppermute | solution.py:404
  113.2 34.6 %collective-permute-start.26 = (bf16[128,1280]{1,0:T(8,128)(2,1)S(1)}, bf16[128,1280]{1,0:T(8,128)(2,1)S(1)}, u32[]{:S(2)}, u32[]{:S(2)}) collective-permute-start(bf16[128,1280]{1,0:T(8,128)(2,1)S(1)} %get-tuple-element.47), channel_id=1, source_target_pairs={{0,96},{32,0},{64,32},{96,64},{1,97},{33,1},{65,33},{97,65},{2,98}... | collective-permute-start | bytes 983048 | tf_op jit(solution)/shard_map/ppermute | solution.py:404
  115.9 32.0 %collective-permute-start.28 = (bf16[128,1280]{1,0:T(8,128)(2,1)S(1)}, bf16[128,1280]{1,0:T(8,128)(2,1)S(1)}, u32[]{:S(2)}, u32[]{:S(2)}) collective-permute-start(bf16[128,1280]{1,0:T(8,128)(2,1)S(1)} %get-tuple-element.49), channel_id=1, source_target_pairs={{0,32},{32,64},{64,96},{96,0},{1,33},{33,65},{65,97},{97,1},{2,34}... | collective-permute-start | bytes 983048 | tf_op jit(solution)/shard_map/ppermute | solution.py:404
  115.9 16.0 %collective-permute-start.17 = (bf16[128,256]{1,0:T(8,128)(2,1)S(1)}, bf16[128,256]{1,0:T(8,128)(2,1)S(1)}, u32[]{:S(2)}, u32[]{:S(2)}) collective-permute-start(bf16[128,256]{1,0:T(8,128)(2,1)S(1)} %add_convert_fusion), channel_id=1, source_target_pairs={{0,16},{4,20},{8,48},{12,52},{16,80},{20,84},{24,112},{28,116},{32... | collective-permute-start | bytes 196616 | tf_op jit(solution)/shard_map/ppermute | solution.py:404
  118.3 18.3 %collective-permute-start.16 = (bf16[128,256]{1,0:T(8,128)(2,1)S(1)}, bf16[128,256]{1,0:T(8,128)(2,1)S(1)}, u32[]{:S(2)}, u32[]{:S(2)}) collective-permute-start(bf16[128,256]{1,0:T(8,128)(2,1)S(1)} %add_convert_fusion), channel_id=1, source_target_pairs={{0,8},{4,12},{8,40},{12,44},{16,72},{20,76},{24,104},{28,108},{32,... | collective-permute-start | bytes 196616 | tf_op jit(solution)/shard_map/ppermute | solution.py:404
  131.8 8.1 %collective-permute-start.15 = (bf16[128,256]{1,0:T(8,128)(2,1)S(1)}, bf16[128,256]{1,0:T(8,128)(2,1)S(1)}, u32[]{:S(2)}, u32[]{:S(2)}) collective-permute-start(bf16[128,256]{1,0:T(8,128)(2,1)S(1)} %add_convert_fusion), channel_id=1, source_target_pairs={{0,0},{4,4},{8,32},{12,36},{16,64},{20,68},{24,96},{28,100},{32,8}... | collective-permute-start | bytes 196616 | tf_op jit(solution)/shard_map/ppermute | solution.py:404
  136.5 5.5 %collective-permute-start.25 = (bf16[128,256]{1,0:T(8,128)(2,1)S(1)}, bf16[128,256]{1,0:T(8,128)(2,1)S(1)}, u32[]{:S(2)}, u32[]{:S(2)}) collective-permute-start(bf16[128,256]{1,0:T(8,128)(2,1)S(1)} %fusion.refs_4_), channel_id=1, source_target_pairs={{0,32},{32,64},{64,96},{96,0},{1,33},{33,65},{65,97},{97,1},{2,34}... | collective-permute-start | bytes 196616 | tf_op jit(solution)/shard_map/ppermute | solution.py:404
  139.9 5.8 %collective-permute-start.24 = (bf16[128,256]{1,0:T(8,128)(2,1)S(1)}, bf16[128,256]{1,0:T(8,128)(2,1)S(1)}, u32[]{:S(2)}, u32[]{:S(2)}) collective-permute-start(bf16[128,256]{1,0:T(8,128)(2,1)S(1)} %fusion.refs_4_), channel_id=1, source_target_pairs={{0,64},{32,96},{64,0},{96,32},{1,65},{33,97},{65,1},{97,33},{2,66}... | collective-permute-start | bytes 196616 | tf_op jit(solution)/shard_map/ppermute | solution.py:404
  142.0 5.8 %collective-permute-start.23 = (bf16[128,256]{1,0:T(8,128)(2,1)S(1)}, bf16[128,256]{1,0:T(8,128)(2,1)S(1)}, u32[]{:S(2)}, u32[]{:S(2)}) collective-permute-start(bf16[128,256]{1,0:T(8,128)(2,1)S(1)} %fusion.refs_4_), channel_id=1, source_target_pairs={{0,96},{32,0},{64,32},{96,64},{1,97},{33,1},{65,33},{97,65},{2,98}... | collective-permute-start | bytes 196616 | tf_op jit(solution)/shard_map/ppermute | solution.py:404
  (11 other events, 193.2 us)
